TPU v7x, 256 devices: a whole 4x4x8 slice. The times are simulated.
256 devices in a mesh: ctx: 32 (over y, z), tp: 8 (over x, core).
Axes of the slice: x: 4, y: 4, z: 8, core: 2. Of those that a mesh axis runs over, the one named last changes fastest.
Arguments:
- context_block_rows: bfloat16 [16384, 8192], P('ctx', 'tp'), may hold values from -16 to 16
- query_hidden_rows: bfloat16 [64, 8192], P(None, 'tp'), may hold values from -16 to 16
- query_token_positions: int32 [64], replicated, may hold values from 16384 to 16573, as said below
- query_bound: int32 [64], replicated, may hold values from 1 to 16384, as said below
- query_matrix: bfloat16 [8192, 8192], P('ctx', 'tp'), may hold values from -0.0625 to 0.0625
- key_matrix: bfloat16 [8192, 1024], P('ctx', 'tp'), may hold values from -0.0625 to 0.0625
- value_matrix: bfloat16 [8192, 1024], P('ctx', 'tp'), may hold values from -0.0625 to 0.0625
Outputs:
- block_out: bfloat16 [16384, 8192], P('ctx', 'tp')
- query_out: bfloat16 [64, 8192], P(None, 'tp')
Inputs may be any that keep to these rules, and one draw needn't show every extreme that they name: query_token_positions rise strictly with the index; the first is 16384 and the last 16573. `query_bound`: some query token sees all 16384 context tokens.
All inputs are finite; a program needn't handle non-finite values.
Results may differ from a plain program's by a relative error of at most 0.0059.
The roundings to bfloat16 on the way count: a program that leaves them out, or rounds other values in their place, can miss the bound.
Values may be sent and summed in bfloat16 or wider, within the bound.
A program may use at most 128 MiB of HBM per device.

v0:
```python
import math
import jax
import jax.numpy as jnp
from jax import lax
from jax.sharding import PartitionSpec as P

HEAD_SIZE = 128


def from_root(value, axis, source):
    kept = jnp.where(lax.axis_index(axis) == source, value, 0).astype(value.dtype)
    return lax.psum(kept, axis)


def rope_table(half):
    values = []
    for index in range(half):
        freq = 500000.0 ** (-2.0 * index / (2.0 * half))
        wavelen = 2.0 * math.pi / freq
        if wavelen > 8192.0:
            values.append(freq / 8.0)
        elif wavelen < 2048.0:
            values.append(freq)
        else:
            smooth = (8192.0 / wavelen - 1.0) / 3.0
            values.append((1.0 - smooth) * freq / 8.0 + smooth * freq)
    return values


def apply_rotary(values, token_positions):
    half = values.shape[-1] // 2
    freqs = jnp.asarray(rope_table(half), jnp.float32)
    angle = token_positions.astype(jnp.float32)[:, None] * freqs[None, :]
    cosine = jnp.cos(angle)[:, None, :]
    sine = jnp.sin(angle)[:, None, :]
    first = values[..., :half]
    second = values[..., half:]
    return jnp.concatenate([first * cosine - second * sine, second * cosine + first * sine], -1)


def attend(query_heads_split, keys, values, valid):
    scale = 1.0 / math.sqrt(query_heads_split.shape[-1])
    scores = (
        jnp.einsum("qkgd,skd->qkgs", query_heads_split, keys, preferred_element_type=jnp.float32)
        * scale
    )
    scores = jnp.where(valid[:, None, None, :], scores, -1e30)
    peak = jnp.max(scores, -1)
    weights = jnp.exp(scores - peak[..., None])
    total = jnp.sum(weights, -1)
    mixed = jnp.einsum(
        "qkgs,skd->qkgd", weights.astype(jnp.bfloat16), values, preferred_element_type=jnp.float32
    )
    return (peak, total, mixed)


def on_device(
    context_block_rows,
    query_hidden_rows,
    query_token_positions,
    query_bound,
    query_matrix,
    key_matrix,
    value_matrix,
):
    ctx_index = lax.axis_index("ctx")
    blk = context_block_rows.shape[0]
    qcount = query_hidden_rows.shape[0]
    heads_q = query_matrix.shape[1] // HEAD_SIZE
    heads_kv = key_matrix.shape[1] // HEAD_SIZE
    head_group = heads_q // heads_kv
    whole_rows, whole_query = (
        lax.all_gather(context_block_rows, "tp", axis=1, tiled=True),
        lax.all_gather(query_hidden_rows, "tp", axis=1, tiled=True),
    )
    stacked = jnp.concatenate([whole_rows, whole_query], 0)
    head_rows = blk + qcount
    proj_query = jnp.dot(
        stacked,
        lax.all_gather(query_matrix, "ctx", axis=0, tiled=True),
        preferred_element_type=jnp.float32,
    )
    proj_key = jnp.dot(
        stacked,
        lax.all_gather(key_matrix, "ctx", axis=0, tiled=True),
        preferred_element_type=jnp.float32,
    )
    proj_value = jnp.dot(
        stacked,
        lax.all_gather(value_matrix, "ctx", axis=0, tiled=True),
        preferred_element_type=jnp.float32,
    )
    local_pos = ctx_index * blk + jnp.arange(blk, dtype=jnp.int32)
    k_block = apply_rotary(proj_key[:blk].reshape(blk, heads_kv, HEAD_SIZE), local_pos).astype(
        jnp.bfloat16
    )
    v_block = proj_value[:blk].reshape(blk, heads_kv, HEAD_SIZE).astype(jnp.bfloat16)
    key_token_rows = apply_rotary(
        proj_key[blk:head_rows].reshape(qcount, heads_kv, HEAD_SIZE), query_token_positions
    ).astype(jnp.bfloat16)
    value_token_rows = (
        proj_value[blk:head_rows].reshape(qcount, heads_kv, HEAD_SIZE).astype(jnp.bfloat16)
    )
    anchor_key, anchor_value = (from_root(k_block, "ctx", 0), from_root(v_block, "ctx", 0))
    q_block = apply_rotary(proj_query[:blk].reshape(blk, heads_q, HEAD_SIZE), local_pos).astype(
        jnp.bfloat16
    )
    query_token_rows = (
        apply_rotary(proj_query[blk:].reshape(qcount, heads_q, HEAD_SIZE), query_token_positions)
        .astype(jnp.bfloat16)
        .reshape(qcount, heads_kv, head_group, HEAD_SIZE)
    )
    keys_cat = jnp.concatenate([anchor_key, k_block], 0)
    values_cat = jnp.concatenate([anchor_value, v_block], 0)
    anchor_live = ctx_index > 0
    rows_step = min(blk, 512)
    rows_here = 0 + jnp.arange(rows_step, dtype=jnp.int32)
    valid = jnp.concatenate(
        [
            jnp.broadcast_to(anchor_live, (rows_step, blk)),
            rows_here[:, None] >= jnp.arange(blk, dtype=jnp.int32)[None, :],
        ],
        1,
    )
    query_heads_split = q_block.reshape(rows_step, heads_kv, head_group, HEAD_SIZE)
    peak, total, mixed = attend(query_heads_split, keys_cat, values_cat, valid)
    outputs = (
        (mixed / total[..., None]).astype(jnp.bfloat16).reshape(rows_step, heads_q * HEAD_SIZE)
    )
    valid_ctx = local_pos[None, :] < query_bound[:, None]
    peak, total, mixed = attend(query_token_rows, k_block, v_block, valid_ctx)
    top = lax.pmax(peak, "ctx")
    scaled = jnp.exp(peak - top)
    total_all, mixed_all = lax.psum((total * scaled, mixed * scaled[..., None]), "ctx")
    own = jnp.arange(qcount, dtype=jnp.int32)
    self_peak, self_total, self_mixed = attend(
        query_token_rows, key_token_rows, value_token_rows, own[:, None] >= own[None, :]
    )
    final = jnp.maximum(top, self_peak)
    w_ctx = jnp.exp(top - final)
    w_self = jnp.exp(self_peak - final)
    query_out = (mixed_all * w_ctx[..., None] + self_mixed * w_self[..., None]) / (
        total_all * w_ctx + self_total * w_self
    )[..., None]
    query_out = query_out.astype(jnp.bfloat16).reshape(qcount, heads_q * HEAD_SIZE)
    return (outputs, query_out)


def solution(mesh):
    placed = (
        P("ctx", "tp"),
        P(None, "tp"),
        P(),
        P(),
        P("ctx", "tp"),
        P("ctx", "tp"),
        P("ctx", "tp"),
    )
    return jax.shard_map(
        on_device,
        mesh=mesh,
        in_specs=placed,
        out_specs=(P("ctx", "tp"), P(None, "tp")),
        check_vma=False,
    )
```

profile of v0, /device:TPU:2, one launch (start us, length us, event | category | flops | bytes accessed | tf_op | source)
XLA Modules:
  0.0 689.7 jit_solution(3943614140132584248)
XLA Ops:
  7.2 0.7 all-gather.6.cloned.1.call-update
  7.9 0.7 all-gather.8.cloned.1.call-update
  8.7 0.7 all-gather.12.cloned.1.call-update
  9.4 0.5 all-gather.10.cloned.1.call-update
  10.0 0.5 all-gather.14.cloned.1.call-update
  10.6 0.7 convert_element_type.69
  11.3 0.1 iota_compare_fusion
  11.3 0.9 concatenate.62
  12.3 1.4 broadcast_compare_fusion
  13.6 0.8 multiply_cosine_fusion.3
  14.5 2.5 multiply_cosine_fusion
  17.0 47.3 %all-gather.6.cloned.1.call-done = bf16[512,8192]{1,0:T(8,128)(2,1)} async-done(((bf16[512,1024]{1,0:T(8,128)(2,1)}), bf16[512,8192]{1,0:T(8,128)(2,1)}) %all-gather.6.cloned.1.call-update) | async-done | bytes 8388624 | tf_op jit(solution)/shard_map/all_gather | solution.py:73
  64.3 7.6 %constant_dynamic-update-slice_fusion.1 = bf16[576,8192]{1,0:T(8,128)(2,1)} fusion(bf16[512,8192]{1,0:T(8,128)(2,1)} %all-gather.6.cloned.1.call-done), kind=kLoop, calls=%fused_computation.100 | loop fusion | bytes 16777216
  71.9 19.5 %all-gather.8.cloned.1.call-done = bf16[64,8192]{1,0:T(8,128)(2,1)} async-done(((bf16[64,1024]{1,0:T(8,128)(2,1)}), bf16[64,8192]{1,0:T(8,128)(2,1)}) %all-gather.8.cloned.1.call-update) | async-done | bytes 1048592 | tf_op jit(solution)/shard_map/all_gather | solution.py:74
  91.4 2.3 constant_dynamic-update-slice_fusion
  93.7 79.8 %all-gather.12.cloned.1.call-done = bf16[8192,128]{1,0:T(8,128)(2,1)} async-done(((bf16[256,128]{1,0:T(8,128)(2,1)}), bf16[8192,128]{1,0:T(8,128)(2,1)}) %all-gather.12.cloned.1.call-update) | async-done | bytes 2097168 | tf_op jit(solution)/shard_map/all_gather | solution.py:85
  173.5 5.8 fusion.83
  179.4 1.2 fusion.35
  180.6 0.8 maximum_select_fusion
  181.4 0.8 fusion.64
  182.2 68.9 %all-gather.10.cloned.1.call-done = bf16[8192,128]{1,0:T(8,128)(2,1)} async-done(((bf16[256,128]{1,0:T(8,128)(2,1)}), bf16[8192,128]{1,0:T(8,128)(2,1)}) %all-gather.10.cloned.1.call-update) | async-done | bytes 2097168 | tf_op jit(solution)/shard_map/all_gather | solution.py:90
  251.1 6.9 convolution_convert_fusion
  258.0 0.7 slice_bitcast_fusion.3
  258.9 132.5 %all-gather.14.cloned.1.call-done = bf16[8192,1024]{1,0:T(8,128)(2,1)} async-done(((bf16[256,1024]{1,0:T(8,128)(2,1)}), bf16[8192,1024]{1,0:T(8,128)(2,1)}) %all-gather.14.cloned.1.call-update) | async-done | bytes 16777232 | tf_op jit(solution)/shard_map/all_gather | solution.py:80
  391.4 14.9 %fusion.84 = f32[576,1024]{1,0:T(8,128)S(1)} fusion(bf16[576,8192]{1,0:T(8,128)(2,1)} %constant_dynamic-update-slice_fusion, bf16[8192,1024]{1,0:T(8,128)(2,1)} %all-gather.14.cloned.1.call-done), kind=kOutput, calls=%fused_computation.126 | convolution fusion | flops 9663676416 | bytes 28573696 | tf_op jit(solution)/shard_map/dot_general | solution.py:78
  406.4 0.1 slice_bitcast_fusion
  406.6 0.1 fusion.80
  406.7 0.1 subtract_convert_fusion.1
  406.8 1.4 fusion.81
  408.2 1.0 fusion.25
  409.1 71.4 %pmax.7 = f32[64,1,8]{0,2,1:T(8,128)S(1)} all-reduce(f32[64,1,8]{0,2,1:T(8,128)S(1)} %bitcast.169), channel_id=1, replica_groups=mesh['ctx'=32,'tp'=8] {'ctx'}, use_global_device_ids=true, to_apply=%region_5.6 | all-reduce | flops 512 | bytes 4096 | tf_op jit(solution)/shard_map/pmax | solution.py:132
  480.6 0.5 copy.38
  481.1 2.0 fusion.79
  483.1 0.6 bitcast_multiply_fusion.1
  483.7 1.1 fusion.14
  484.8 3.5 subtract_convert_fusion
  488.2 47.8 %all-reduce.7.cloned.1.call-done = (bf16[512,1,128]{2,0,1:T(8,128)(2,1)}, bf16[512,1,128]{2,0,1:T(8,128)(2,1)}) async-done(((bf16[512,1,128]{2,0,1:T(8,128)(2,1)}, bf16[512,1,128]{2,0,1:T(8,128)(2,1)}), (bf16[512,1,128]{2,0,1:T(8,128)(2,1)}, bf16[512,1,128]{2,0,1:T(8,128)(2,1)})) %all-reduce.7.cloned.1.call-update) | async-done | bytes 262160 | tf_op jit(solution)/shard_map/psum | solution.py:12
  536.1 10.7 %fusion.2 = (f32[512,8]{0,1:T(8,128)S(1)}, f32[1024,512,8]{1,0,2:T(8,128)}) fusion(pred[512,1024]{0,1:T(8,128)(4,1)} %concatenate.62, bf16[512,8,64]{2,0,1:T(8,128)(2,1)} %get-tuple-element.9, bf16[512,8,64]{2,0,1:T(8,128)(2,1)S(1)} %get-tuple-element.8, bf16[512,1,64]{2,0,1:T(8,128)(2,1)} %copy-done.1, bf16[512,1,64]{2,0,1:T(8,128)(2,1)S(1)} %get-tuple-element.14, ...), kind=kOutput, calls=%fused_computation.4 | convolution fusion | flops 1089204224 | bytes 18628608 | tf_op jit(solution)/shard_map/qkgd,skd->qkgs/dot_general | solution.py:44
  546.8 9.3 %fusion = f32[512,8]{0,1:T(8,128)S(1)} fusion(f32[1024,512,8]{1,0,2:T(8,128)} %get-tuple-element.32, f32[512,8]{0,1:T(8,128)S(1)} %get-tuple-element.31, pred[512,1024]{0,1:T(8,128)(4,1)S(1)} %copy-done), kind=kLoop, calls=%fused_computation.2 | loop fusion | flops 16773120 | bytes 17334272 | tf_op jit(solution)/shard_map/reduce_sum | solution.py:50
  556.1 0.3 fusion.82
  556.5 9.1 %fusion.7 = bf16[1,128,512,8]{2,1,3,0:T(8,128)(2,1)S(1)} fusion(f32[1024,512,8]{1,0,2:T(8,128)} %get-tuple-element.32, f32[512,8]{0,1:T(8,128)S(1)} %get-tuple-element.31, pred[512,1024]{0,1:T(8,128)(4,1)S(1)} %copy-done, f32[512,8]{0,1:T(8,128)S(1)} %fusion, bf16[512,1,128]{2,0,1:T(8,128)(2,1)S(1)} %copy-done.4, bf16[512,1,128]{2,0,1:T(8,128)(2,1)S(1)} %copy-done.10), kind=kOutput, calls=%fused_computation.10 | convolution fusion | flops 1092091904 | bytes 18644992 | tf_op jit(solution)/shard_map/qkgs,skd->qkgd/dot_general | solution.py:51
  565.6 0.1 fusion.44
  565.7 1.3 copy.29
  567.0 72.5 %psum.31 = f32[64,1,8]{0,2,1:T(8,128)S(1)} all-reduce(f32[64,1,8]{0,2,1:T(8,128)S(1)} %copy-done.8), channel_id=1, replica_groups=mesh['ctx'=32,'tp'=8] {'ctx'}, use_global_device_ids=true, to_apply=%region_9.10 | all-reduce | flops 512 | bytes 4096 | tf_op jit(solution)/shard_map/psum | solution.py:134
  639.5 41.2 %all-reduce.5.cloned.1.call-done = f32[64,1,8,128]{3,0,2,1:T(8,128)} async-done(((f32[64,1,8,128]{3,0,2,1:T(8,128)}), f32[64,1,8,128]{3,0,2,1:T(8,128)}) %all-reduce.5.cloned.1.call-update) | async-done | bytes 262160 | tf_op jit(solution)/shard_map/psum | solution.py:134
  680.7 1.3 fusion.19
  682.0 0.1 copy.28
  682.1 0.7 copy.50
  (39 shorter events, 0.5 us)
Async XLA Ops:
  7.2 57.1 %all-gather.6.cloned.1.call-start = ((), (), s32[]{:S(2)}) async-start(), calls=%async_computation | async-start | bytes 9437184 | tf_op jit(solution)/shard_map/all_gather | solution.py:73
  7.9 83.5 %all-gather.8.cloned.1.call-start = ((), (), s32[]{:S(2)}) async-start(), calls=%async_computation.1 | async-start | bytes 1179648 | tf_op jit(solution)/shard_map/all_gather | solution.py:74
  8.6 164.9 %all-gather.12.cloned.1.call-start = ((), (), s32[]{:S(2)}) async-start(), calls=%async_computation.3 | async-start | bytes 2162688 | tf_op jit(solution)/shard_map/all_gather | solution.py:85
  9.4 241.7 %all-gather.10.cloned.1.call-start = ((), (), s32[]{:S(2)}) async-start(), calls=%async_computation.2 | async-start | bytes 2162688 | tf_op jit(solution)/shard_map/all_gather | solution.py:90
  10.0 381.4 %all-gather.14.cloned.1.call-start = ((), (), s32[]{:S(2)}) async-start(), calls=%async_computation.4 | async-start | bytes 17301504 | tf_op jit(solution)/shard_map/all_gather | solution.py:80
  10.5 525.5 %all-reduce.7.cloned.1.call-start = ((), (), s32[]{:S(2)}) async-start(), calls=%async_computation.6 | async-start | bytes 524288 | tf_op jit(solution)/shard_map/psum | solution.py:12
  71.9 107.5 %copy-start.9 = (f32[64]{0:T(128)S(1)}, f32[64]{0:T(128)}, u32[]{:S(2)}) copy-start(f32[64]{0:T(128)} %constant.24.clone) | copy-start | bytes 772
  180.6 225.7 %copy-start.1 = (bf16[512,1,64]{2,0,1:T(8,128)(2,1)}, bf16[512,1,64]{2,0,1:T(8,128)(2,1)S(1)}, u32[]{:S(2)}) copy-start(bf16[512,1,64]{2,0,1:T(8,128)(2,1)S(1)} %get-tuple-element.15) | copy-start | bytes 196612
  258.0 133.4 %copy-start.2 = (bf16[576,128]{1,0:T(8,128)(2,1)}, bf16[576,128]{1,0:T(8,128)(2,1)S(1)}, u32[]{:S(2)}) copy-start(bf16[576,128]{1,0:T(8,128)(2,1)S(1)} %convolution_convert_fusion) | copy-start | bytes 442372
  258.8 421.9 %all-reduce.5.cloned.1.call-start = ((), (), s32[]{:S(2)}) async-start(), calls=%async_computation.5 | async-start | bytes 524288 | tf_op jit(solution)/shard_map/psum | solution.py:134
  480.6 2.5 copy-start.7
  480.6 3.1 copy-start.3
  536.1 10.7 %copy-start = (pred[512,1024]{0,1:T(8,128)(4,1)S(1)}, pred[512,1024]{0,1:T(8,128)(4,1)}, u32[]{:S(2)}) copy-start(pred[512,1024]{0,1:T(8,128)(4,1)} %concatenate.62) | copy-start | bytes 1572868
  546.8 9.3 %copy-start.5 = (bf16[64,64]{1,0:T(8,128)(2,1)S(1)}, bf16[64,64]{1,0:T(8,128)(2,1)}, u32[]{:S(2)}) copy-start(bf16[64,64]{1,0:T(8,128)(2,1)} %get-tuple-element.20) | copy-start | bytes 24580
  546.8 9.3 %copy-start.6 = (bf16[64,64]{1,0:T(8,128)(2,1)S(1)}, bf16[64,64]{1,0:T(8,128)(2,1)}, u32[]{:S(2)}) copy-start(bf16[64,64]{1,0:T(8,128)(2,1)} %get-tuple-element.21) | copy-start | bytes 24580
  546.8 9.6 %copy-start.4 = (bf16[512,1,128]{2,0,1:T(8,128)(2,1)S(1)}, bf16[512,1,128]{2,0,1:T(8,128)(2,1)}, u32[]{:S(2)}) copy-start(bf16[512,1,128]{2,0,1:T(8,128)(2,1)} %get-tuple-element.18) | copy-start | bytes 393220
  546.8 9.6 %copy-start.10 = (bf16[512,1,128]{2,0,1:T(8,128)(2,1)S(1)}, bf16[512,1,128]{2,0,1:T(8,128)(2,1)}, u32[]{:S(2)}) copy-start(bf16[512,1,128]{2,0,1:T(8,128)(2,1)} %get-tuple-element.7) | copy-start | bytes 393220
  556.5 10.5 %copy-start.8 = (f32[64,1,8]{0,2,1:T(8,128)S(1)}, f32[64,1,8]{0,2,1:T(8,128)}, u32[]{:S(2)}) copy-start(f32[64,1,8]{0,2,1:T(8,128)} %get-tuple-element.25) | copy-start | bytes 6148
Sparse Core Ops, SparseCore 0:
  9.8 54.4 all-gather.5
  66.1 25.2 all-gather.7
  94.0 79.4 all-gather.11
  176.0 75.1 all-gather.9
  253.6 137.7 all-gather.13
  394.7 141.2 all-reduce.6
  539.5 141.1 all-reduce.4
where the time goes:
time: 690 us
  waiting for transfers between devices  440 us (64%)
  blocking collectives  144 us (21%)
  matrix products  51.5 us (7%)
  other arithmetic  23.5 us (3%)
  local copies, waits for them, and re-layouts  15.8 us (2%)
  between operations  14.4 us (2%)
    all_gather x1, waiting for transfers between devices, on_device(): lax.all_gather(query_matrix, 'ctx', axis=0, tiled=True)  133 us
    all_gather x1, waiting for transfers between devices, on_device(): lax.all_gather(key_matrix, 'ctx', axis=0, tiled=True)  79.8 us
    psum x1, blocking collectives, on_device(): lax.psum((total * scaled, mixed * scaled[..., None]), 'ctx')  72.5 us
    pmax x1, blocking collectives, on_device(): top = lax.pmax(peak, 'ctx')  71.4 us
    all_gather x1, waiting for transfers between devices, on_device(): lax.all_gather(value_matrix, 'ctx', axis=0, tiled=True)  68.9 us
    psum x1, waiting for transfers between devices, from_root(): return lax.psum(kept, axis)  47.8 us
    all_gather x1, waiting for transfers between devices, on_device(): lax.all_gather(context_block_rows, 'tp', axis=1, tiled=True)  47.3 us
    psum x1, waiting for transfers between devices, on_device(): lax.psum((total * scaled, mixed * scaled[..., None]), 'ctx')  41.2 us
  transfers between devices with their start and end apart: 7, of which 7 were waited for; matrix products, arithmetic and copies ran while one was open for 13% of the time, Pallas kernels for 0%

commit v1 on v0

--- a/solution.py
+++ b/solution.py
@@ -9,7 +9,7 @@
 
 def from_root(value, axis, source):
     kept = jnp.where(lax.axis_index(axis) == source, value, 0).astype(value.dtype)
-    return lax.psum(kept, axis)
+    return jnp.sum(lax.all_gather(kept, axis), axis=0)
 
 
 def rope_table(half):

time: 690 us -> 794 us (1.15)
  waiting for transfers between devices: 440 us -> 547 us
    all_gather x0 -> x2, waiting for transfers between devices: none -> 146 us  [from_root(): return jnp.sum(lax.all_gather(kept, axis), axis=0)]
    psum x1 -> x0, waiting for transfers between devices: 47.8 us -> none  [from_root(): return lax.psum(kept, axis)]
    all_gather x1, waiting for transfers between devices: 68.9 us -> 79.8 us  [on_device(): lax.all_gather(value_matrix, 'ctx', axis=0, tiled=True)]
    all_gather x1, waiting for transfers between devices: 79.8 us -> 69.2 us  [on_device(): lax.all_gather(key_matrix, 'ctx', axis=0, tiled=True)]
  transfers between devices with their start and end apart: 7 -> 8, of which waited for: 7 -> 8; matrix products, arithmetic and copies ran while one was open for 13% -> 8% of each run, Pallas kernels for 0% -> 0%
where the time goes in v1:
time: 794 us
  waiting for transfers between devices  547 us (69%)
  blocking collectives  141 us (18%)
  matrix products  49.2 us (6%)
  other arithmetic  25.7 us (3%)
  local copies, waits for them, and re-layouts  15.1 us (2%)
  between operations  14.5 us (2%)
    all_gather x2, waiting for transfers between devices, from_root(): return jnp.sum(lax.all_gather(kept, axis), axis=0)  146 us
    all_gather x1, waiting for transfers between devices, on_device(): lax.all_gather(query_matrix, 'ctx', axis=0, tiled=True)  137 us
    all_gather x1, waiting for transfers between devices, on_device(): lax.all_gather(value_matrix, 'ctx', axis=0, tiled=True)  79.8 us
    pmax x1, blocking collectives, on_device(): top = lax.pmax(peak, 'ctx')  71.4 us
    psum x1, blocking collectives, on_device(): lax.psum((total * scaled, mixed * scaled[..., None]), 'ctx')  70.1 us
    all_gather x1, waiting for transfers between devices, on_device(): lax.all_gather(key_matrix, 'ctx', axis=0, tiled=True)  69.2 us
    all_gather x1, waiting for transfers between devices, on_device(): lax.all_gather(context_block_rows, 'tp', axis=1, tiled=True)  54.3 us
    psum x1, waiting for transfers between devices, on_device(): lax.psum((total * scaled, mixed * scaled[..., None]), 'ctx')  38.3 us
  transfers between devices with their start and end apart: 8, of which 8 were waited for; matrix products, arithmetic and copies ran while one was open for 8% of the time, Pallas kernels for 0%

profile of v1, /device:TPU:2, one launch (start us, length us, event | category | flops | bytes accessed | tf_op | source)
XLA Modules:
  0.0 793.9 jit_solution(241551781261374322)
XLA Ops:
  7.2 0.7 all-gather.9.cloned.1.call-update
  7.9 0.7 all-gather.11.cloned.1.call-update
  8.7 0.7 all-gather.13.cloned.1.call-update
  9.4 0.5 all-gather.15.cloned.1.call-update
  10.0 54.3 %all-gather.9.cloned.1.call-done = bf16[512,8192]{1,0:T(8,128)(2,1)} async-done(((bf16[512,1024]{1,0:T(8,128)(2,1)}), bf16[512,8192]{1,0:T(8,128)(2,1)}) %all-gather.9.cloned.1.call-update) | async-done | bytes 8388624 | tf_op jit(solution)/shard_map/all_gather | solution.py:73
  64.3 7.6 constant_dynamic-update-slice_fusion.1
  71.9 19.5 %all-gather.11.cloned.1.call-done = bf16[64,8192]{1,0:T(8,128)(2,1)} async-done(((bf16[64,1024]{1,0:T(8,128)(2,1)}), bf16[64,8192]{1,0:T(8,128)(2,1)}) %all-gather.11.cloned.1.call-update) | async-done | bytes 1048592 | tf_op jit(solution)/shard_map/all_gather | solution.py:74
  91.4 2.4 constant_dynamic-update-slice_fusion
  93.7 79.8 %all-gather.13.cloned.1.call-done = bf16[8192,128]{1,0:T(8,128)(2,1)} async-done(((bf16[256,128]{1,0:T(8,128)(2,1)}), bf16[8192,128]{1,0:T(8,128)(2,1)}) %all-gather.13.cloned.1.call-update) | async-done | bytes 2097168 | tf_op jit(solution)/shard_map/all_gather | solution.py:90
  173.5 7.0 convolution_convert_fusion
  180.5 0.6 copy-done.5
  181.1 0.7 broadcast_select_fusion
  181.9 69.2 %all-gather.15.cloned.1.call-done = bf16[8192,128]{1,0:T(8,128)(2,1)} async-done(((bf16[256,128]{1,0:T(8,128)(2,1)}), bf16[8192,128]{1,0:T(8,128)(2,1)}) %all-gather.15.cloned.1.call-update) | async-done | bytes 2097168 | tf_op jit(solution)/shard_map/all_gather | solution.py:85
  251.1 5.8 fusion.83
  257.0 1.2 fusion.35
  258.2 0.8 maximum_select_fusion
  259.1 0.7 all-gather.19.cloned.1.call-update
  259.8 0.2 all-reduce.3.cloned.1.call-start
  260.1 0.9 concatenate.73
  261.0 0.7 broadcast_compare_fusion
  261.7 0.2 multiply_cosine_fusion.3
  261.9 1.8 multiply_cosine_fusion
  263.7 0.8 fusion.64
  264.5 68.1 %all-gather.21.cloned.1.call-done = bf16[16384,128]{1,0:T(8,128)(2,1)} async-done(((bf16[512,128]{1,0:T(8,128)(2,1)}), bf16[16384,128]{1,0:T(8,128)(2,1)}) %all-gather.21.cloned.1.call-update) | async-done | bytes 4194320 | tf_op jit(solution)/shard_map/all_gather | solution.py:12
  332.6 3.5 reduce.10
  336.1 78.1 %all-gather.17.cloned.1.call-done = bf16[32,512,1,128]{3,1,2,0:T(8,128)(2,1)} async-done(((bf16[1,512,1,128]{3,1,2,0:T(8,128)(2,1)}), bf16[32,512,1,128]{3,1,2,0:T(8,128)(2,1)}) %all-gather.17.cloned.1.call-update) | async-done | bytes 4194320 | tf_op jit(solution)/shard_map/all_gather | solution.py:12
  414.1 3.4 reduce_sum.61
  417.6 137.0 %all-gather.19.cloned.1.call-done = bf16[8192,1024]{1,0:T(8,128)(2,1)} async-done(((bf16[256,1024]{1,0:T(8,128)(2,1)}), bf16[8192,1024]{1,0:T(8,128)(2,1)}) %all-gather.19.cloned.1.call-update) | async-done | bytes 16777232 | tf_op jit(solution)/shard_map/all_gather | solution.py:80
  554.6 14.9 %fusion.84 = f32[576,1024]{1,0:T(8,128)S(1)} fusion(bf16[576,8192]{1,0:T(8,128)(2,1)} %constant_dynamic-update-slice_fusion, bf16[8192,1024]{1,0:T(8,128)(2,1)} %all-gather.19.cloned.1.call-done), kind=kOutput, calls=%fused_computation.126 | convolution fusion | flops 9663676416 | bytes 28573696 | tf_op jit(solution)/shard_map/dot_general | solution.py:78
  569.6 0.1 slice_bitcast_fusion
  569.8 0.1 fusion.80
  570.0 1.4 fusion.81
  571.4 0.9 fusion.25
  572.3 71.4 %pmax.7 = f32[64,1,8]{0,2,1:T(8,128)S(1)} all-reduce(f32[64,1,8]{0,2,1:T(8,128)S(1)} %bitcast.177), channel_id=1, replica_groups=mesh['ctx'=32,'tp'=8] {'ctx'}, use_global_device_ids=true, to_apply=%region_5.6 | all-reduce | flops 512 | bytes 4096 | tf_op jit(solution)/shard_map/pmax | solution.py:132
  643.8 1.3 bitcast_multiply_fusion.1
  645.0 2.0 fusion.14
  647.0 0.5 copy.47
  647.6 0.7 fusion.79
  648.2 0.8 subtract_convert_fusion
  649.1 7.6 fusion.2
  656.7 9.3 %fusion = f32[512,8]{0,1:T(8,128)S(1)} fusion(f32[1024,512,8]{1,0,2:T(8,128)} %get-tuple-element.32, f32[512,8]{0,1:T(8,128)S(1)} %get-tuple-element.31, pred[512,1024]{0,1:T(8,128)(4,1)S(1)} %copy-done), kind=kLoop, calls=%fused_computation.2 | loop fusion | flops 16773120 | bytes 17334272 | tf_op jit(solution)/shard_map/reduce_sum | solution.py:50
  666.0 0.3 fusion.82
  666.4 8.9 %fusion.7 = bf16[1,128,512,8]{2,1,3,0:T(8,128)(2,1)S(1)} fusion(f32[1024,512,8]{1,0,2:T(8,128)} %get-tuple-element.32, f32[512,8]{0,1:T(8,128)S(1)} %get-tuple-element.31, pred[512,1024]{0,1:T(8,128)(4,1)S(1)} %copy-done, f32[512,8]{0,1:T(8,128)S(1)} %fusion, bf16[512,1,128]{2,0,1:T(8,128)(2,1)S(1)} %copy-done.9, bf16[512,1,128]{2,0,1:T(8,128)(2,1)S(1)} %bitcast.174), kind=kOutput, calls=%fused_computation.10 | convolution fusion | flops 1092091904 | bytes 18644992 | tf_op jit(solution)/shard_map/qkgs,skd->qkgd/dot_general | solution.py:51
  675.3 1.3 copy.38
  676.6 70.1 %psum.15 = f32[64,1,8]{0,2,1:T(8,128)S(1)} all-reduce(f32[64,1,8]{0,2,1:T(8,128)S(1)} %copy-done.12), channel_id=1, replica_groups=mesh['ctx'=32,'tp'=8] {'ctx'}, use_global_device_ids=true, to_apply=%region_9.10 | all-reduce | flops 512 | bytes 4096 | tf_op jit(solution)/shard_map/psum | solution.py:134
  746.7 38.3 %all-reduce.3.cloned.1.call-done = f32[64,1,8,128]{3,0,2,1:T(8,128)} async-done(((f32[64,1,8,128]{3,0,2,1:T(8,128)}), f32[64,1,8,128]{3,0,2,1:T(8,128)}) %all-reduce.3.cloned.1.call-update) | async-done | bytes 262160 | tf_op jit(solution)/shard_map/psum | solution.py:134
  785.0 1.3 fusion.19
  786.4 0.7 copy.59
  (54 shorter events, 0.9 us)
Async XLA Ops:
  7.2 57.1 %all-gather.9.cloned.1.call-start = ((), (), s32[]{:S(2)}) async-start(), calls=%async_computation | async-start | bytes 9437184 | tf_op jit(solution)/shard_map/all_gather | solution.py:73
  7.9 83.5 %all-gather.11.cloned.1.call-start = ((), (), s32[]{:S(2)}) async-start(), calls=%async_computation.1 | async-start | bytes 1179648 | tf_op jit(solution)/shard_map/all_gather | solution.py:74
  8.6 164.9 %all-gather.13.cloned.1.call-start = ((), (), s32[]{:S(2)}) async-start(), calls=%async_computation.2 | async-start | bytes 2162688 | tf_op jit(solution)/shard_map/all_gather | solution.py:90
  9.4 241.7 %all-gather.15.cloned.1.call-start = ((), (), s32[]{:S(2)}) async-start(), calls=%async_computation.3 | async-start | bytes 2162688 | tf_op jit(solution)/shard_map/all_gather | solution.py:85
  10.0 322.7 %all-gather.21.cloned.1.call-start = ((), (), s32[]{:S(2)}) async-start(), calls=%async_computation.7 | async-start | bytes 4325376 | tf_op jit(solution)/shard_map/all_gather | solution.py:12
  180.5 0.7 copy-start.5
  181.1 75.8 %copy-start.13 = (f32[64]{0:T(128)S(1)}, f32[64]{0:T(128)}, u32[]{:S(2)}) copy-start(f32[64]{0:T(128)} %constant.26.clone) | copy-start | bytes 772
  181.1 78.9 %copy-start.15 = (s32[64]{0:T(128)S(1)}, s32[64]{0:T(128)}, u32[]{:S(2)}) copy-start(s32[64]{0:T(128)} %param.13) | copy-start | bytes 772
  181.9 79.1 %copy-start.14 = (s32[64]{0:T(128)S(1)}, s32[64]{0:T(128)}, u32[]{:S(2)}) copy-start(s32[64]{0:T(128)} %param.14) | copy-start | bytes 772
  181.9 232.2 %all-gather.17.cloned.1.call-start = ((), (), s32[]{:S(2)}) async-start(), calls=%async_computation.4 | async-start | bytes 4325376 | tf_op jit(solution)/shard_map/all_gather | solution.py:12
  258.2 311.3 %copy-start.1 = (bf16[512,1,64]{2,0,1:T(8,128)(2,1)}, bf16[512,1,64]{2,0,1:T(8,128)(2,1)S(1)}, u32[]{:S(2)}) copy-start(bf16[512,1,64]{2,0,1:T(8,128)(2,1)S(1)} %get-tuple-element.15) | copy-start | bytes 196612
  259.0 295.6 %all-gather.19.cloned.1.call-start = ((), (), s32[]{:S(2)}) async-start(), calls=%async_computation.5 | async-start | bytes 17301504 | tf_op jit(solution)/shard_map/all_gather | solution.py:80
  259.8 525.2 %all-reduce.3.cloned.1.call-start = ((), (), s32[]{:S(2)}) async-start(), calls=%async_computation.6 | async-start | bytes 524288 | tf_op jit(solution)/shard_map/psum | solution.py:134
  554.6 15.4 %copy-start.8 = (pred[64,512]{1,0:T(8,128)(4,1)S(1)}, pred[64,512]{1,0:T(8,128)(4,1)}, u32[]{:S(2)}) copy-start(pred[64,512]{1,0:T(8,128)(4,1)} %broadcast_compare_fusion) | copy-start | bytes 98308
  647.0 1.2 copy-start.3
  647.0 1.2 copy-start.4
  647.5 1.5 copy-start
  647.5 1.5 copy-start.2
  647.5 1.5 copy-start.7
  656.7 9.3 %copy-start.10 = (bf16[64,64]{1,0:T(8,128)(2,1)S(1)}, bf16[64,64]{1,0:T(8,128)(2,1)}, u32[]{:S(2)}) copy-start(bf16[64,64]{1,0:T(8,128)(2,1)} %get-tuple-element.20) | copy-start | bytes 24580
  656.7 9.3 %copy-start.11 = (bf16[64,64]{1,0:T(8,128)(2,1)S(1)}, bf16[64,64]{1,0:T(8,128)(2,1)}, u32[]{:S(2)}) copy-start(bf16[64,64]{1,0:T(8,128)(2,1)} %get-tuple-element.21) | copy-start | bytes 24580
  656.7 9.6 %copy-start.6 = (bf16[512,128]{1,0:T(8,128)(2,1)S(1)}, bf16[512,128]{1,0:T(8,128)(2,1)}, u32[]{:S(2)}) copy-start(bf16[512,128]{1,0:T(8,128)(2,1)} %reduce.10) | copy-start | bytes 393220
  656.7 9.6 %copy-start.9 = (bf16[512,1,128]{2,0,1:T(8,128)(2,1)S(1)}, bf16[512,1,128]{2,0,1:T(8,128)(2,1)}, u32[]{:S(2)}) copy-start(bf16[512,1,128]{2,0,1:T(8,128)(2,1)} %get-tuple-element.19) | copy-start | bytes 393220
  666.4 10.3 %copy-start.12 = (f32[64,1,8]{0,2,1:T(8,128)S(1)}, f32[64,1,8]{0,2,1:T(8,128)}, u32[]{:S(2)}) copy-start(f32[64,1,8]{0,2,1:T(8,128)} %get-tuple-element.25) | copy-start | bytes 6148
Sparse Core Ops, SparseCore 0:
  9.8 54.4 all-gather.8
  66.1 25.2 all-gather.10
  94.0 79.4 all-gather.12
  175.9 75.1 all-gather.14
  253.6 79.0 all-gather.20
  335.1 79.0 all-gather.16
  416.7 137.8 all-gather.18
  647.2 137.8 all-reduce.2
